TPU v7x, 32 devices: a whole 2x2x4 slice. The times are simulated.
32 devices in a mesh: illum: 16 (over z, y, x), row: 2 (over core).
Axes of the slice: x: 2, y: 2, z: 4, core: 2. Of those that a mesh axis runs over, the one named last changes fastest.
Arguments:
- angles: int32 [64, 2], P('illum'), may hold values from -8 to 8
- depth_order: int32 [3], replicated, may hold values from 0 to 15, as said below
- slices: float32 [16, 16, 4096], P('illum', 'row'), may hold values from -4 to 4
- cotangent: float32 [64, 2, 16, 4096], P('illum', None, 'row'), may hold values from -0.6 to 0.6
Outputs:
- exit_field: float32 [64, 2, 16, 4096], P('illum', None, 'row')
- slice_grad: float32 [16, 16, 4096], P('illum', 'row')
Inputs may be any that keep to these rules, and one draw needn't show every extreme that they name: `depth_order`: 3 distinct slice numbers; slice 0 and the last slice are always among them.
All inputs are finite; a program needn't handle non-finite values.
Results may differ from a plain program's by a relative error of at most 0.0001.
Values sent between devices are 32-bit elements; how exact they have to be, the bound alone decides.
A program may use at most 64 MiB of HBM per device.

v0:
```python
import math

import jax
import jax.numpy as jnp
from jax import lax
from jax.sharding import PartitionSpec as P

rate_scale = 0.3


def extended(array, sides, width):
    for axis, dim in sides:
        peers, length = (lax.axis_size(axis), array.shape[dim])
        up = [(i, (i + 1) % peers) for i in range(peers - 1)]
        down = [(j, i) for i, j in up]
        last = lax.slice_in_dim(array, length - width, length, axis=dim)
        initial = lax.slice_in_dim(array, 0, width, axis=dim)
        before = lax.ppermute(last, axis, up)
        after = lax.ppermute(initial, axis, down)
        array = jnp.concatenate([before, array, after], axis=dim)
    return array


def broadcast(block, axis, holder):
    block = jnp.where(lax.axis_index(axis) == holder, block, jnp.zeros_like(block))
    return lax.psum(block, axis)


def laplace_whole(field):
    framed = jnp.pad(field, ((0, 0), (0, 0), (1, 1), (1, 1)))
    return (
        framed[:, :, 2:, 1:-1]
        + framed[:, :, :-2, 1:-1]
        + (framed[:, :, 1:-1, 2:] + framed[:, :, 1:-1, :-2])
        - 4.0 * field
    )


def deep_runge(field, factor, valid):
    padded = extended(field, (("row", 2),), 4)

    def slope(state):
        curved = laplace_whole(state)
        return jnp.stack([-factor * curved[:, 1], factor * curved[:, 0]], axis=1) * valid

    slope_one = slope(padded)
    slope_two = slope(padded + 0.5 * slope_one)
    slope_three = slope(padded + 0.5 * slope_two)
    slope_four = slope(padded + slope_three)
    total = padded + (slope_one + 2.0 * slope_two + 2.0 * slope_three + slope_four) / 6.0
    return total[:, :, 4:-4]


def rotate(field, phase):
    cosine = jnp.cos(phase)
    sine = jnp.sin(phase)
    real_part = field[:, 0]
    imag_part = field[:, 1]
    return jnp.stack(
        [cosine * real_part - sine * imag_part, sine * real_part + cosine * imag_part], axis=1
    )


def inner_term(adjoint, stored):
    return jnp.sum(-adjoint[:, 0] * stored[:, 1] + adjoint[:, 1] * stored[:, 0], axis=0)


def body(angles, depth_order, slices, cotangent):
    rows = slices.shape[1]
    cols = slices.shape[2]
    layers = depth_order.shape[0]
    owner_count = lax.axis_size("illum")
    total_rows = rows * lax.axis_size("row")
    first_row = lax.axis_index("row") * rows
    rows_idx = first_row + jnp.arange(rows, dtype=jnp.int32)
    cols_idx = jnp.arange(cols, dtype=jnp.int32)
    phase_rows = (
        2.0
        * math.pi
        * (angles[:, 0:1] * rows_idx[None, :] % total_rows).astype(jnp.float32)
        / total_rows
    )
    phase_cols = (
        2.0 * math.pi * (angles[:, 1:2] * cols_idx[None, :] % cols).astype(jnp.float32) / cols
    )
    phase = phase_rows[:, :, None] + phase_cols[:, None, :]
    field = jnp.stack([jnp.cos(phase), jnp.sin(phase)], axis=1)
    chosen = [broadcast(slices[0], "illum", depth_order[layer]) for layer in range(layers)]
    kept = [None] * layers
    terms = [None] * layers
    adjoint = cotangent
    wide_idx = first_row - 4 + jnp.arange(rows + 8, dtype=jnp.int32)
    valid = ((wide_idx >= 0) & (wide_idx < total_rows)).astype(jnp.float32)[:, None]
    for layer in range(layers):
        field = rotate(field, chosen[layer])
        kept[layer] = field
        field = deep_runge(field, rate_scale, valid)
    for layer in range(layers - 1, -1, -1):
        adjoint = deep_runge(adjoint, -rate_scale, valid)
        terms[layer] = inner_term(adjoint, kept[layer])
        adjoint = rotate(adjoint, -chosen[layer])
    grads = jnp.stack(terms, axis=0)
    owners = jnp.arange(owner_count, dtype=jnp.int32)
    buffer = jnp.zeros((owner_count, rows, cols), jnp.float32)
    for layer in range(layers):
        picked = (owners == depth_order[layer]).astype(jnp.float32)
        buffer = buffer + picked[:, None, None] * grads[layer][None]
    slice_grad = lax.psum_scatter(buffer, "illum", scatter_dimension=0, tiled=True)
    return (field, slice_grad)


def solution(mesh):
    placed = (P("illum", None), P(), P("illum", "row", None), P("illum", None, "row", None))
    return jax.shard_map(
        body,
        mesh=mesh,
        in_specs=placed,
        out_specs=(P("illum", None, "row", None), P("illum", "row", None)),
        check_vma=False,
    )
```

profile of v0, /device:TPU:0, one launch (start us, length us, event | category | flops | bytes accessed | tf_op | source)
XLA Modules:
  0.0 301.2 jit_solution(4131242680538914036)
XLA Ops:
  7.2 2.6 fusion.163
  9.8 2.4 collective-permute-start.6
  12.2 1.3 collective-permute-start.7
  17.8 1.3 compare_convert_fusion
  19.1 109.6 %all-reduce.27.cloned.1.call-done = (f32[8,4096]{1,0:T(8,128)}, f32[8,4096]{1,0:T(8,128)}, f32[8,4096]{1,0:T(8,128)}) async-done(((f32[8,4096]{1,0:T(8,128)}, f32[8,4096]{1,0:T(8,128)}, f32[8,4096]{1,0:T(8,128)}), (f32[8,4096]{1,0:T(8,128)}, f32[8,4096]{1,0:T(8,128)}, f32[8,4096]{1,0:T(8,128)})) %all-reduce.27.cloned.1.call-update) | async-done | bytes 393232 | tf_op jit(solution)/shard_map/psum | solution.py:26
  128.8 1.4 fusion.164
  130.2 1.8 negate_cosine_fusion.1
  132.0 2.0 fusion.136
  134.2 1.3 collective-permute-start
  135.5 1.5 collective-permute-start.1
  138.4 1.1 fusion.50
  140.4 1.1 fusion.54
  142.3 1.1 fusion.58
  144.3 1.1 fusion.62
  145.7 1.3 fusion.105
  147.3 3.1 %collective-permute-start.8 = (f32[4,2,4,4096]{3,2,0,1:T(4,128)S(1)}, f32[4,2,4,4096]{3,2,0,1:T(4,128)S(1)}, u32[]{:S(2)}, u32[]{:S(2)}) collective-permute-start(f32[4,2,4,4096]{3,2,0,1:T(4,128)S(1)} %get-tuple-element.59), channel_id=1, source_target_pairs={{0,1},{2,3},{4,5},{6,7},{8,9},{10,11},{12,13},{14,15},{16,17},{18,... | collective-permute-start | bytes 1572872 | tf_op jit(solution)/shard_map/ppermute | solution.py:18
  150.4 1.7 collective-permute-start.9
  152.5 1.1 fusion.2
  154.6 1.1 fusion.66
  156.6 1.1 fusion.70
  157.9 1.3 multiply_add_fusion.4
  159.2 2.3 fusion.6
  162.0 1.7 fusion.110
  163.7 1.1 fusion.78
  166.2 2.8 collective-permute-start.10
  168.9 1.3 collective-permute-start.11
  172.1 1.1 fusion.14
  173.5 1.3 fusion.98
  175.1 3.1 %collective-permute-start.2 = (f32[4,2,4,4096]{3,2,0,1:T(4,128)S(1)}, f32[4,2,4,4096]{3,2,0,1:T(4,128)S(1)}, u32[]{:S(2)}, u32[]{:S(2)}) collective-permute-start(f32[4,2,4,4096]{3,2,0,1:T(4,128)S(1)} %get-tuple-element.65), channel_id=1, source_target_pairs={{0,1},{2,3},{4,5},{6,7},{8,9},{10,11},{12,13},{14,15},{16,17},{18,... | collective-permute-start | bytes 1572872 | tf_op jit(solution)/shard_map/ppermute | solution.py:18
  178.2 1.5 collective-permute-start.3
  181.2 1.1 fusion.82
  186.9 1.1 fusion.94
  189.6 1.1 fusion.18
  191.5 1.1 fusion.22
  193.7 1.1 fusion.26
  195.6 2.5 fusion.30
  198.1 1.7 slice_multiply_fusion.27
  199.8 1.3 fusion.101
  202.3 1.2 fusion.108
  203.6 2.5 fusion.133
  207.1 3.1 %collective-permute-start.4 = (f32[4,2,4,4096]{3,2,0,1:T(4,128)}, f32[4,2,4,4096]{3,2,0,1:T(4,128)S(1)}, u32[]{:S(2)}, u32[]{:S(2)}) collective-permute-start(f32[4,2,4,4096]{3,2,0,1:T(4,128)} %get-tuple-element.63), channel_id=1, source_target_pairs={{0,1},{2,3},{4,5},{6,7},{8,9},{10,11},{12,13},{14,15},{16,17},{18,... | collective-permute-start | bytes 1572872 | tf_op jit(solution)/shard_map/ppermute | solution.py:18
  210.1 1.5 collective-permute-start.5
  211.7 1.8 multiply_add_fusion
  214.3 1.1 fusion.34
  218.3 1.1 fusion.42
  220.2 1.1 fusion.46
  222.3 1.2 fusion.115
  223.6 70.5 %reduce-scatter.2.cloned.1.call-done = f32[1,8,4096]{2,1,0:T(8,128)} async-done(((f32[16,8,4096]{2,1,0:T(8,128)}), f32[1,8,4096]{2,1,0:T(8,128)}) %reduce-scatter.2.cloned.1.call-update) | async-done | bytes 131088 | tf_op jit(solution)/shard_map/reduce_scatter | solution.py:108
  (106 shorter events, 30.8 us)
Async XLA Ops:
  7.2 6.3 %copy-start.7 = (s32[3]{0:T(128)S(1)}, s32[3]{0:T(128)}, u32[]{:S(2)}) copy-start(s32[3]{0:T(128)} %param.5) | copy-start | bytes 40
  7.2 8.9 %copy-start.5 = (f32[1,8,4096]{2,1,0:T(8,128)S(1)}, f32[1,8,4096]{2,1,0:T(8,128)}, u32[]{:S(2)}) copy-start(f32[1,8,4096]{2,1,0:T(8,128)} %param.6) | copy-start | bytes 393220
  7.2 10.4 %copy-start.8 = (s32[4,2]{0,1:T(2,128)S(1)}, s32[4,2]{0,1:T(2,128)}, u32[]{:S(2)}) copy-start(s32[4,2]{0,1:T(2,128)} %param.4) | copy-start | bytes 100
  7.2 121.6 %all-reduce.27.cloned.1.call-start = ((), (), s32[]{:S(2)}) async-start(), calls=%async_computation.2 | async-start | bytes 786432 | tf_op jit(solution)/shard_map/psum | solution.py:26
  9.8 128.1 %collective-permute-start.6 = (f32[4,2,4,4096]{3,2,0,1:T(4,128)}, f32[4,2,4,4096]{3,2,0,1:T(4,128)S(1)}, u32[]{:S(2)}, u32[]{:S(2)}) collective-permute-start(f32[4,2,4,4096]{3,2,0,1:T(4,128)} %get-tuple-element.61), channel_id=1, source_target_pairs={{0,1},{2,3},{4,5},{6,7},{8,9},{10,11},{12,13},{14,15},{16,17},{18,... | collective-permute-start | bytes 1572872 | tf_op jit(solution)/shard_map/ppermute | solution.py:18
  12.2 125.8 %collective-permute-start.7 = (f32[4,2,4,4096]{3,2,0,1:T(4,128)S(1)}, f32[4,2,4,4096]{3,2,0,1:T(4,128)S(1)}, u32[]{:S(2)}, u32[]{:S(2)}) collective-permute-start(f32[4,2,4,4096]{3,2,0,1:T(4,128)S(1)} %get-tuple-element.62), channel_id=1, source_target_pairs={{1,0},{3,2},{5,4},{7,6},{9,8},{11,10},{13,12},{15,14},{17,16},{19,... | collective-permute-start | bytes 1572872 | tf_op jit(solution)/shard_map/ppermute | solution.py:19
  16.9 277.2 %reduce-scatter.2.cloned.1.call-start = ((), (), s32[]{:S(2)}) async-start(), calls=%async_computation.1 | async-start | bytes 2228224 | tf_op jit(solution)/shard_map/reduce_scatter | solution.py:108
  17.7 116.5 %copy-start.2 = (f32[4,4096]{1,0:T(4,128)}, f32[4,4096]{1,0:T(4,128)S(1)}, u32[]{:S(2)}) copy-start(f32[4,4096]{1,0:T(4,128)S(1)} %fusion.159) | copy-start | bytes 196612
  130.1 6.9 %copy-start.6 = (f32[8,4096]{1,0:T(8,128)S(1)}, f32[8,4096]{1,0:T(8,128)}, u32[]{:S(2)}) copy-start(f32[8,4096]{1,0:T(8,128)} %get-tuple-element.4) | copy-start | bytes 393220
  132.0 6.0 %copy-start = (f32[4,2,8,4096]{3,2,1,0:T(8,128)S(1)}, f32[4,2,8,4096]{3,2,1,0:T(8,128)}, u32[]{:S(2)}) copy-start(f32[4,2,8,4096]{3,2,1,0:T(8,128)} %param.7) | copy-start | bytes 3145732
  134.2 18.0 %collective-permute-start = (f32[4,2,4,4096]{3,2,0,1:T(4,128)S(1)}, f32[4,2,4,4096]{3,2,0,1:T(4,128)S(1)}, u32[]{:S(2)}, u32[]{:S(2)}) collective-permute-start(f32[4,2,4,4096]{3,2,0,1:T(4,128)S(1)} %get-tuple-element.67), channel_id=1, source_target_pairs={{0,1},{2,3},{4,5},{6,7},{8,9},{10,11},{12,13},{14,15},{16,17},{18,... | collective-permute-start | bytes 1572872 | tf_op jit(solution)/shard_map/ppermute | solution.py:18
  135.5 16.6 %collective-permute-start.1 = (f32[4,2,4,4096]{3,2,0,1:T(4,128)S(1)}, f32[4,2,4,4096]{3,2,0,1:T(4,128)S(1)}, u32[]{:S(2)}, u32[]{:S(2)}) collective-permute-start(f32[4,2,4,4096]{3,2,0,1:T(4,128)S(1)} %get-tuple-element.68), channel_id=1, source_target_pairs={{1,0},{3,2},{5,4},{7,6},{9,8},{11,10},{13,12},{15,14},{17,16},{19,... | collective-permute-start | bytes 1572872 | tf_op jit(solution)/shard_map/ppermute | solution.py:19
  147.3 6.6 %collective-permute-start.8 = (f32[4,2,4,4096]{3,2,0,1:T(4,128)S(1)}, f32[4,2,4,4096]{3,2,0,1:T(4,128)S(1)}, u32[]{:S(2)}, u32[]{:S(2)}) collective-permute-start(f32[4,2,4,4096]{3,2,0,1:T(4,128)S(1)} %get-tuple-element.59), channel_id=1, source_target_pairs={{0,1},{2,3},{4,5},{6,7},{8,9},{10,11},{12,13},{14,15},{16,17},{18,... | collective-permute-start | bytes 1572872 | tf_op jit(solution)/shard_map/ppermute | solution.py:18
  150.4 3.8 %collective-permute-start.9 = (f32[4,2,4,4096]{3,2,0,1:T(4,128)S(1)}, f32[4,2,4,4096]{3,2,0,1:T(4,128)S(1)}, u32[]{:S(2)}, u32[]{:S(2)}) collective-permute-start(f32[4,2,4,4096]{3,2,0,1:T(4,128)S(1)} %get-tuple-element.60), channel_id=1, source_target_pairs={{1,0},{3,2},{5,4},{7,6},{9,8},{11,10},{13,12},{15,14},{17,16},{19,... | collective-permute-start | bytes 1572872 | tf_op jit(solution)/shard_map/ppermute | solution.py:19
  166.2 14.6 %collective-permute-start.10 = (f32[4,2,4,4096]{3,2,0,1:T(4,128)S(1)}, f32[4,2,4,4096]{3,2,0,1:T(4,128)S(1)}, u32[]{:S(2)}, u32[]{:S(2)}) collective-permute-start(f32[4,2,4,4096]{3,2,0,1:T(4,128)S(1)} %get-tuple-element.57), channel_id=1, source_target_pairs={{0,1},{2,3},{4,5},{6,7},{8,9},{10,11},{12,13},{14,15},{16,17},{18,... | collective-permute-start | bytes 1572872 | tf_op jit(solution)/shard_map/ppermute | solution.py:18
  168.9 11.9 %collective-permute-start.11 = (f32[4,2,4,4096]{3,2,0,1:T(4,128)S(1)}, f32[4,2,4,4096]{3,2,0,1:T(4,128)S(1)}, u32[]{:S(2)}, u32[]{:S(2)}) collective-permute-start(f32[4,2,4,4096]{3,2,0,1:T(4,128)S(1)} %get-tuple-element.58), channel_id=1, source_target_pairs={{1,0},{3,2},{5,4},{7,6},{9,8},{11,10},{13,12},{15,14},{17,16},{19,... | collective-permute-start | bytes 1572872 | tf_op jit(solution)/shard_map/ppermute | solution.py:19
  175.1 14.1 %collective-permute-start.2 = (f32[4,2,4,4096]{3,2,0,1:T(4,128)S(1)}, f32[4,2,4,4096]{3,2,0,1:T(4,128)S(1)}, u32[]{:S(2)}, u32[]{:S(2)}) collective-permute-start(f32[4,2,4,4096]{3,2,0,1:T(4,128)S(1)} %get-tuple-element.65), channel_id=1, source_target_pairs={{0,1},{2,3},{4,5},{6,7},{8,9},{10,11},{12,13},{14,15},{16,17},{18,... | collective-permute-start | bytes 1572872 | tf_op jit(solution)/shard_map/ppermute | solution.py:18
  178.2 11.0 %collective-permute-start.3 = (f32[4,2,4,4096]{3,2,0,1:T(4,128)S(1)}, f32[4,2,4,4096]{3,2,0,1:T(4,128)S(1)}, u32[]{:S(2)}, u32[]{:S(2)}) collective-permute-start(f32[4,2,4,4096]{3,2,0,1:T(4,128)S(1)} %get-tuple-element.66), channel_id=1, source_target_pairs={{1,0},{3,2},{5,4},{7,6},{9,8},{11,10},{13,12},{15,14},{17,16},{19,... | collective-permute-start | bytes 1572872 | tf_op jit(solution)/shard_map/ppermute | solution.py:19
  201.1 1.2 copy-start.1
  202.3 1.3 copy-start.3
  203.6 8.1 %copy-start.4 = (f32[8,4096]{1,0:T(8,128)S(1)}, f32[8,4096]{1,0:T(8,128)}, u32[]{:S(2)}) copy-start(f32[8,4096]{1,0:T(8,128)} %fusion.151) | copy-start | bytes 393220
  207.1 6.4 %collective-permute-start.4 = (f32[4,2,4,4096]{3,2,0,1:T(4,128)}, f32[4,2,4,4096]{3,2,0,1:T(4,128)S(1)}, u32[]{:S(2)}, u32[]{:S(2)}) collective-permute-start(f32[4,2,4,4096]{3,2,0,1:T(4,128)} %get-tuple-element.63), channel_id=1, source_target_pairs={{0,1},{2,3},{4,5},{6,7},{8,9},{10,11},{12,13},{14,15},{16,17},{18,... | collective-permute-start | bytes 1572872 | tf_op jit(solution)/shard_map/ppermute | solution.py:18
  210.1 3.8 %collective-permute-start.5 = (f32[4,2,4,4096]{3,2,0,1:T(4,128)S(1)}, f32[4,2,4,4096]{3,2,0,1:T(4,128)S(1)}, u32[]{:S(2)}, u32[]{:S(2)}) collective-permute-start(f32[4,2,4,4096]{3,2,0,1:T(4,128)S(1)} %get-tuple-element.64), channel_id=1, source_target_pairs={{1,0},{3,2},{5,4},{7,6},{9,8},{11,10},{13,12},{15,14},{17,16},{19,... | collective-permute-start | bytes 1572872 | tf_op jit(solution)/shard_map/ppermute | solution.py:19
Sparse Core Ops, SparseCore 0:
  17.0 111.7 all-reduce.26
  213.6 80.4 reduce-scatter.1
where the time goes:
time: 305 us; the launch traced here: 301 us
  waiting for transfers between devices  181 us (59%)
  other arithmetic  73.3 us (24%)
  starting transfers between devices  24.6 us (8%)
  between operations  17.1 us (6%)
  local copies, waits for them, and re-layouts  5.23 us (2%)
    psum x1, waiting for transfers between devices, broadcast(): return lax.psum(block, axis)  110 us
    reduce_scatter x1, waiting for transfers between devices, body(): lax.psum_scatter(buffer, 'illum', scatter_dimension=0, tiled=True)  70.5 us
    sub x23, other arithmetic, laplace_whole(): framed[:, :, 2:, 1:-1] + framed[:, :, :-2, 1:-1]  28.9 us
    ppermute x6, starting transfers between devices, extended(): before = lax.ppermute(last, axis, up)  15.7 us
    ppermute x6, starting transfers between devices, extended(): after = lax.ppermute(initial, axis, down)  8.76 us
    mul x24, other arithmetic, slope(): -factor * curved[:, 1]  7.21 us
    add x6, other arithmetic, deep_runge(): padded + (slope_one + 2.0 * slope_two + 2.0 * slope_three + slope_four) /...  6.97 us
  transfers between devices with their start and end apart: 14, of which 4 were waited for; matrix products, arithmetic and copies ran while one was open for 15% of the time, Pallas kernels for 0%

commit v1 on v0

--- a/solution.py
+++ b/solution.py
@@ -1,8 +1,11 @@
+import functools
 import math
 
 import jax
 import jax.numpy as jnp
 from jax import lax
+from jax.experimental import pallas as pl
+from jax.experimental.pallas import tpu as pltpu
 from jax.sharding import PartitionSpec as P
 
 rate_scale = 0.3
@@ -109,10 +112,425 @@
     return (field, slice_grad)
 
 
+MESH = pl.DeviceIdType.MESH
+PAD = 128
+STRIP = 512
+
+
+def sincos(x):
+    k = jnp.floor(x * (2.0 / math.pi) + 0.5)
+    r = x - k * 1.5703125
+    r = r - k * 4.837512969970703125e-4
+    r = r - k * 7.54978995489188e-8
+    z = r * r
+    s = r + r * z * (-1.6666654611e-1 + z * (8.3321608736e-3 - z * 1.9515295891e-4))
+    c = 1.0 - 0.5 * z + z * z * (
+        4.166664568298827e-2 + z * (-1.388731625493765e-3 + z * 2.443315711809948e-5)
+    )
+    q = k.astype(jnp.int32) & 3
+    odd = (q & 1) == 1
+    sin_mag = jnp.where(odd, c, s)
+    cos_mag = jnp.where(odd, s, c)
+    sine = jnp.where(q >= 2, -sin_mag, sin_mag)
+    cosine = jnp.where((q == 1) | (q == 2), -cos_mag, cos_mag)
+    return sine, cosine
+
+
+def propagate(source, target, g, factor, cols):
+    wide = STRIP + 2 * PAD
+    sub = lax.broadcasted_iota(jnp.int32, (8, wide), 0)
+    lane = lax.broadcasted_iota(jnp.int32, (8, wide), 1)
+    first, final = sub == 0, sub == 7
+    second = factor * factor / 2.0
+    third = factor * factor * factor / 6.0
+    fourth = factor * factor * factor * factor / 24.0
+    mid = slice(PAD, PAD + STRIP)
+
+    def strip(j, carry):
+        start = pl.multiple_of(j * STRIP, STRIP)
+        col = lane + (start - PAD)
+        inside = jnp.where((col >= 0) & (col < cols), 1.0, 0.0).astype(jnp.float32)
+
+        def curved(t, b):
+            rt, rb = pltpu.roll(t, 1, 0), pltpu.roll(b, 1, 0)
+            qt, qb = pltpu.roll(t, 7, 0), pltpu.roll(b, 7, 0)
+            vt = jnp.where(first, 0.0, rt) + jnp.where(final, qb, qt)
+            vb = jnp.where(first, rt, rb) + jnp.where(final, 0.0, qb)
+            ht = pltpu.roll(t, 1, 1) + pltpu.roll(t, wide - 1, 1)
+            hb = pltpu.roll(b, 1, 1) + pltpu.roll(b, wide - 1, 1)
+            return (vt + ht) - 4.0 * t, (vb + hb) - 4.0 * b
+
+        evens, odds = [], []
+        for part in range(2):
+            u0 = source[g, part, 0:8, pl.ds(start, wide)]
+            u1 = source[g, part, 8:16, pl.ds(start, wide)]
+            a0, a1 = curved(u0, u1)
+            a0, a1 = a0 * inside, a1 * inside
+            b0, b1 = curved(a0, a1)
+            b0, b1 = b0 * inside, b1 * inside
+            even = [u[:, mid] - second * b[:, mid] for u, b in ((u0, b0), (u1, b1))]
+            c0, c1 = curved(b0, b1)
+            c0, c1 = c0 * inside, c1 * inside
+            odd = [factor * a[:, mid] - third * c[:, mid] for a, c in ((a0, c0), (a1, c1))]
+            d0, d1 = curved(c0, c1)
+            even = [e + fourth * d[:, mid] for e, d in zip(even, (d0, d1))]
+            evens.append(even)
+            odds.append(odd)
+        for half in range(2):
+            at = slice(8 * half, 8 * half + 8)
+            target[g, 0, at, pl.ds(start, STRIP)] = evens[0][half] - odds[1][half]
+            target[g, 1, at, pl.ds(start, STRIP)] = evens[1][half] + odds[0][half]
+        return carry
+
+    lax.fori_loop(0, cols // STRIP, strip, 0)
+
+
+def fused(
+    count, angles, order, slices, cot, out, grad,
+    tmp, w2, w1, w0, field, full, sine, cosine, term, got, total, parts, rs, picks, gfull, pieces,
+    cot_send, cot_recv, cot_local, a2a_send, a2a_recv, ag_send, ag_recv, cx_send, cx_recv,
+    tx_send, tx_recv, rs_send, rs_recv, fin_send, fin_recv, ex_send, ex_recv, ex_local,
+):
+    n = count
+    me = lax.axis_index("illum")
+    core = lax.axis_index("row")
+    other = 1 - core
+    cols = slices.shape[1]
+    width = cols // n
+    held = cot.shape[0] // 2
+    layers = full.shape[0]
+    mine_rows = pl.ds(pl.multiple_of(core * 8, 8), 8)
+    other_rows = pl.ds(pl.multiple_of(other * 8, 8), 8)
+    my_cols = pl.ds(pl.multiple_of(me * width, width), width)
+
+    def peer(k):
+        return lax.rem(me + k, n)
+
+    def piece(k):
+        return pl.ds(pl.multiple_of(k * width, width), width)
+
+    def loop(body):
+        def step(k, carry):
+            body(k)
+            return carry
+
+        lax.fori_loop(1, n, step, 0)
+
+    barrier = pltpu.get_barrier_semaphore()
+    loop(lambda k: pl.semaphore_signal(barrier, inc=1, device_id=(peer(k), core), device_id_type=MESH))
+    pl.semaphore_signal(barrier, inc=1, device_id=(me, other), device_id_type=MESH)
+    pl.semaphore_wait(barrier, n)
+
+    def remote(src, dst, send, recv, where):
+        return pltpu.make_async_remote_copy(
+            src_ref=src, dst_ref=dst, send_sem=send, recv_sem=recv,
+            device_id=where, device_id_type=MESH,
+        )
+
+    inner = pl.ds(PAD, cols)
+
+    def cot_copy(g):
+        return remote(
+            cot.at[other * held + g], tmp.at[g, :, mine_rows, inner],
+            cot_send.at[g], cot_recv.at[g], (me, other),
+        )
+
+    def cot_own(g):
+        return pltpu.make_async_copy(
+            cot.at[core * held + g], tmp.at[g, :, mine_rows, inner], cot_local.at[g]
+        )
+
+    def a2a(k):
+        return remote(
+            slices.at[:, piece(peer(k))], parts.at[me], a2a_send.at[k], a2a_recv.at[k],
+            (peer(k), core),
+        )
+
+    def gather(layer, k):
+        return remote(
+            pieces.at[layer], full.at[layer, mine_rows, my_cols],
+            ag_send.at[layer, k], ag_recv.at[layer, k], (peer(k), core),
+        )
+
+    def cross(layer):
+        return remote(
+            full.at[layer, mine_rows], full.at[layer, mine_rows],
+            cx_send.at[layer], cx_recv.at[layer], (me, other),
+        )
+
+    def term_copy(layer):
+        return remote(
+            term.at[layer, other_rows], got.at[layer],
+            tx_send.at[layer], tx_recv.at[layer], (me, other),
+        )
+
+    def scatter(layer, k):
+        return remote(
+            total.at[layer, :, piece(peer(k))], rs.at[layer, k],
+            rs_send.at[layer, k], rs_recv.at[layer, k], (peer(k), core),
+        )
+
+    def final(k):
+        to = peer(k)
+        which = (to + n - 2) // (n - 1) + to // (n - 1)
+        return remote(
+            picks.at[which], gfull.at[:, my_cols], fin_send.at[k], fin_recv.at[k], (to, core)
+        )
+
+    def exit_copy(g):
+        return remote(
+            field.at[g, :, other_rows], out.at[core * held + g],
+            ex_send.at[g], ex_recv.at[g], (me, other),
+        )
+
+    def exit_own(g):
+        return pltpu.make_async_copy(
+            field.at[g, :, mine_rows], out.at[core * held + g], ex_local.at[g]
+        )
+
+    for g in range(held):
+        cot_copy(g).start()
+        cot_own(g).start()
+    loop(lambda k: a2a(k).start())
+    parts[me] = slices[:, my_cols]
+    for g in range(held):
+        for part in range(2):
+            tmp[g, part, :, 0:PAD] = jnp.zeros((16, PAD), jnp.float32)
+            tmp[g, part, :, PAD + cols : 2 * PAD + cols] = jnp.zeros((16, PAD), jnp.float32)
+
+    def back_first(g):
+        cot_copy(g).wait_recv()
+        cot_own(g).wait()
+        propagate(tmp, w2, g, -rate_scale, cols)
+
+    back_first(0)
+    loop(lambda k: a2a(k).wait_recv())
+    for layer in range(layers - 1, -1, -1):
+        value = parts[order[layer]]
+        pieces[layer] = value
+        full[layer, mine_rows, my_cols] = value
+        loop(lambda k: gather(layer, k).start())
+    for g in range(1, held):
+        back_first(g)
+
+    def fetch(layer):
+        loop(lambda k: gather(layer, k).wait_recv())
+        cross(layer).start()
+
+    tile = 512
+
+    def columns(body):
+        def step(j, carry):
+            body(pl.multiple_of(j * tile, tile))
+            return carry
+
+        lax.fori_loop(0, cols // tile, step, 0)
+
+    def back_turn(layer, waves):
+        def body(start):
+            at = pl.ds(start, tile)
+            to = pl.ds(start + PAD, tile)
+            s, c = sincos(full[layer, :, at])
+            sine[layer, :, at] = s
+            cosine[layer, :, at] = c
+            for g in range(held):
+                a, b = waves[g, 0, :, at], waves[g, 1, :, at]
+                tmp[g, 0, :, to] = a * c + b * s
+                tmp[g, 1, :, to] = b * c - a * s
+
+        columns(body)
+
+    fetch(2)
+    cross(2).wait_recv()
+    fetch(1)
+    back_turn(2, w2)
+    for g in range(held):
+        propagate(tmp, w1, g, -rate_scale, cols)
+    cross(1).wait_recv()
+    fetch(0)
+    back_turn(1, w1)
+    for g in range(held):
+        propagate(tmp, w0, g, -rate_scale, cols)
+    cross(0).wait_recv()
+
+    def first_turn(start):
+        at = pl.ds(start, tile)
+        to = pl.ds(start + PAD, tile)
+        phase = full[0, :, at]
+        row = lax.broadcasted_iota(jnp.int32, (16, tile), 0)
+        col = lax.broadcasted_iota(jnp.int32, (16, tile), 1) + start
+        acc = None
+        for g in range(held):
+            p = angles[core * held + g, 0]
+            q = angles[core * held + g, 1]
+            turn = ((row * p) & 15).astype(jnp.float32) * (2.0 * math.pi / 16)
+            turn = turn + ((col * q) & (cols - 1)).astype(jnp.float32) * (2.0 * math.pi / cols)
+            s, c = sincos(turn + phase)
+            tmp[g, 0, :, to] = c
+            tmp[g, 1, :, to] = s
+            piece_sum = w0[g, 1, :, at] * c - w0[g, 0, :, at] * s
+            acc = piece_sum if acc is None else acc + piece_sum
+        term[0, :, at] = acc
+
+    def turn(layer, waves):
+        def body(start):
+            at = pl.ds(start, tile)
+            to = pl.ds(start + PAD, tile)
+            s, c = sine[layer, :, at], cosine[layer, :, at]
+            acc = None
+            for g in range(held):
+                a, b = field[g, 0, :, at], field[g, 1, :, at]
+                real = a * c - b * s
+                imag = a * s + b * c
+                tmp[g, 0, :, to] = real
+                tmp[g, 1, :, to] = imag
+                piece_sum = waves[g, 1, :, at] * real - waves[g, 0, :, at] * imag
+                acc = piece_sum if acc is None else acc + piece_sum
+            term[layer, :, at] = acc
+
+        columns(body)
+
+    def spread(layer):
+        term_copy(layer).wait_recv()
+        total[layer] = term[layer, mine_rows] + got[layer]
+        loop(lambda k: scatter(layer, k).start())
+
+    columns(first_turn)
+    term_copy(0).start()
+    propagate(tmp, field, 0, rate_scale, cols)
+    spread(0)
+    for g in range(1, held):
+        propagate(tmp, field, g, rate_scale, cols)
+    turn(1, w1)
+    term_copy(1).start()
+    propagate(tmp, field, 0, rate_scale, cols)
+    spread(1)
+    for g in range(1, held):
+        propagate(tmp, field, g, rate_scale, cols)
+    turn(2, w2)
+    term_copy(2).start()
+    propagate(tmp, field, 0, rate_scale, cols)
+    spread(2)
+    exit_copy(0).start()
+    exit_own(0).start()
+    for g in range(1, held):
+        propagate(tmp, field, g, rate_scale, cols)
+        exit_copy(g).start()
+        exit_own(g).start()
+
+    sums = []
+    for layer in range(layers):
+        loop(lambda k: scatter(layer, k).wait_recv())
+        acc = total[layer, :, my_cols]
+        for k in range(1, n):
+            acc = acc + rs[layer, k]
+        sums.append(acc)
+    zero = jnp.zeros_like(sums[0])
+    low = zero
+    high = zero
+    middle = zero
+    for layer in range(layers):
+        place = order[layer]
+        low = low + jnp.where(place == 0, sums[layer], zero)
+        high = high + jnp.where(place == n - 1, sums[layer], zero)
+        middle = middle + jnp.where((place > 0) & (place < n - 1), sums[layer], zero)
+    picks[0] = low
+    picks[1] = middle
+    picks[2] = high
+    loop(lambda k: final(k).start())
+    gfull[:, my_cols] = picks[(me + n - 2) // (n - 1) + me // (n - 1)]
+    named = (order[0] == me) | (order[1] == me) | (order[2] == me)
+    loop(lambda k: final(k).wait_recv())
+    value = gfull[...]
+    grad[...] = jnp.where(named, value, jnp.zeros_like(value))
+
+    for g in range(held):
+        cot_copy(g).wait_send()
+        exit_own(g).wait()
+        exit_copy(g).wait()
+
+    def drain(k):
+        a2a(k).wait_send()
+        final(k).wait_send()
+        for layer in range(layers):
+            gather(layer, k).wait_send()
+            scatter(layer, k).wait_send()
+
+    loop(drain)
+    for layer in range(layers):
+        cross(layer).wait_send()
+        term_copy(layer).wait_send()
+
+
+def fast_body(angles, depth_order, slices, cotangent):
+    count = lax.axis_size("illum")
+    _, rows, cols = slices.shape
+    groups = cotangent.shape[0]
+    held = groups // 2
+    layers = depth_order.shape[0]
+    width = cols // count
+    dma = pltpu.SemaphoreType.DMA
+    f32 = jnp.float32
+    wave = pltpu.VMEM((held, 2, 2 * rows, cols), f32)
+    plane = pltpu.VMEM((layers, 2 * rows, cols), f32)
+    half_plane = pltpu.VMEM((layers, rows, cols), f32)
+    vmem = pl.BlockSpec(memory_space=pltpu.VMEM)
+    smem = pl.BlockSpec(memory_space=pltpu.SMEM)
+    out, grad = pl.pallas_call(
+        functools.partial(fused, count),
+        out_shape=(
+            jax.ShapeDtypeStruct(cotangent.shape, f32),
+            jax.ShapeDtypeStruct((rows, cols), f32),
+        ),
+        in_specs=[smem, smem, vmem, vmem],
+        out_specs=(pl.BlockSpec(memory_space=pl.ANY), vmem),
+        scratch_shapes=[
+            pltpu.VMEM((held, 2, 2 * rows, cols + 2 * PAD), f32),
+            wave, wave, wave, wave,
+            plane, plane, plane, plane, half_plane, half_plane,
+            pltpu.VMEM((count, rows, width), f32),
+            pltpu.VMEM((layers, count, rows, width), f32),
+            pltpu.VMEM((3, rows, width), f32),
+            pltpu.VMEM((rows, cols), f32),
+            pltpu.VMEM((layers, rows, width), f32),
+            dma((held,)), dma((held,)), dma((held,)),
+            dma((count,)), dma((count,)),
+            dma((layers, count)), dma((layers, count)),
+            dma((layers,)), dma((layers,)),
+            dma((layers,)), dma((layers,)),
+            dma((layers, count)), dma((layers, count)),
+            dma((count,)), dma((count,)),
+            dma((held,)), dma((held,)), dma((held,)),
+        ],
+        compiler_params=pltpu.CompilerParams(
+            collective_id=0, has_side_effects=True, vmem_limit_bytes=40 * 1024 * 1024
+        ),
+    )(angles, depth_order, slices[0], cotangent)
+    return out, grad[None]
+
+
+def chosen_body(angles, depth_order, slices, cotangent):
+    count = lax.axis_size("illum")
+    _, rows, cols = slices.shape
+    fits = (
+        lax.axis_size("row") == 2
+        and rows == 8
+        and slices.shape[0] == 1
+        and count >= 3
+        and cotangent.shape[0] % 2 == 0
+        and depth_order.shape[0] == 3
+        and cols & (cols - 1) == 0
+        and cols % (128 * count) == 0
+        and cols % 512 == 0
+    )
+    run = fast_body if fits else body
+    return run(angles, depth_order, slices, cotangent)
+
+
 def solution(mesh):
     placed = (P("illum", None), P(), P("illum", "row", None), P("illum", None, "row", None))
     return jax.shard_map(
-        body,
+        chosen_body,
         mesh=mesh,
         in_specs=placed,
         out_specs=(P("illum", None, "row", None), P("illum", "row", None)),

time: 305 us -> 69.1 us (0.23); the launches traced: 301 us -> 68.9 us
  waiting for transfers between devices: 181 us -> 0 us
  other arithmetic: 73.3 us -> 0 us
  Pallas kernels: 0 us -> 63.2 us
  starting transfers between devices: 24.6 us -> 0 us
  between operations: 17.1 us -> 0.65 us
    psum x1 -> x0, waiting for transfers between devices: 110 us -> none  [broadcast(): return lax.psum(block, axis)]
    reduce_scatter x1 -> x0, waiting for transfers between devices: 70.5 us -> none  [body(): lax.psum_scatter(buffer, 'illum', scatter_dimension=0, tiled=True)]
    pallas_call x0 -> x1, Pallas kernels: none -> 63.2 us  [fast_body(): pl.pallas_call(functools.partial(fused, count), out_shape=(jax.ShapeDtype...]
    sub x28 -> x0, other arithmetic: 31.7 us -> none  [the longest x23 28.9 us: laplace_whole(): framed[:, :, 2:, 1:-1] + framed[:, :, :-2, 1:-1]]
    ppermute x12 -> x0, starting transfers between devices: 24.5 us -> none  [the longest x6 15.7 us: extended(): before = lax.ppermute(last, axis, up)]
    add x25 -> x0, other arithmetic: 20.7 us -> none  [the longest x6 6.97 us: deep_runge(): padded + (slope_one + 2.0 * slope_two + 2.0 * slope_three + slope_four) /...]
    mul x27 -> x0, other arithmetic: 7.49 us -> none  [the longest x24 7.21 us: slope(): -factor * curved[:, 1]]
    unnamed x18 -> x11, local copies, waits for them, and re-layouts: 0.65 us -> 5.08 us
  transfers between devices with their start and end apart: 14 -> 0, of which waited for: 4 -> 0; matrix products, arithmetic and copies ran while one was open for 15% -> 0% of each run, Pallas kernels for 0% -> 0%
where the time goes in v1:
time: 69.1 us; the launch traced here: 68.9 us
  Pallas kernels  63.2 us (91%)
  local copies, waits for them, and re-layouts  5.08 us (7%)
    pallas_call x1, Pallas kernels, fast_body(): pl.pallas_call(functools.partial(fused, count), out_shape=(jax.ShapeDtype...  63.2 us
    unnamed x11, local copies, waits for them, and re-layouts  5.08 us

profile of v1, /device:TPU:0, one launch (start us, length us, event | category | flops | bytes accessed | tf_op | source)
XLA Modules:
  0.0 68.9 jit_solution(3432126057573686202)
XLA Ops:
  0.6 0.0 copy-start.3
  0.6 0.7 copy-done.3
  1.3 0.0 copy-start.2
  1.3 0.1 copy.6.angles
  1.4 0.6 copy-done.2
  2.0 0.0 copy-start
  2.0 1.2 %copy-done = f32[4,2,8,4096]{3,2,1,0:T(8,128)S(1)} copy-done((f32[4,2,8,4096]{3,2,1,0:T(8,128)S(1)}, f32[4,2,8,4096]{3,2,1,0:T(8,128)}, u32[]{:S(2)}) %copy-start) | copy-done | bytes 1048600
  3.2 0.0 copy-start.1
  3.2 0.9 %copy-done.1 = f32[1,8,4096]{2,1,0:T(8,128)S(1)} copy-done((f32[1,8,4096]{2,1,0:T(8,128)S(1)}, f32[1,8,4096]{2,1,0:T(8,128)}, u32[]{:S(2)}) %copy-start.1) | copy-done | bytes 131096
  4.1 63.2 %shard_map.59 = (f32[4,2,8,4096]{3,2,1,0:T(8,128)S(1)}, f32[8,4096]{1,0:T(8,128)S(1)}) custom-call(s32[4,2]{1,0:T(4,128)S(1)} %copy.6.angles, s32[3]{0:T(128)S(1)} %copy-done.2, f32[8,4096]{1,0:T(8,128)S(1)} %bitcast.2, f32[4,2,8,4096]{3,2,1,0:T(8,128)S(1)} %copy-done), custom_call_target="tpu_custom_call" | custom-call | tf_op jit(solution)/shard_map/pallas_call | solution.py:479
  67.3 1.0 %copy.9 = f32[4,2,8,4096]{3,2,1,0:T(8,128)} copy(f32[4,2,8,4096]{3,2,1,0:T(8,128)S(1)} %get-tuple-element.8) | data formatting | bytes 2097152
  68.3 0.7 copy.10
Async XLA Ops:
  0.6 0.7 copy-start.3
  1.3 0.7 copy-start.2
  2.0 1.2 %copy-start = (f32[4,2,8,4096]{3,2,1,0:T(8,128)S(1)}, f32[4,2,8,4096]{3,2,1,0:T(8,128)}, u32[]{:S(2)}) copy-start(f32[4,2,8,4096]{3,2,1,0:T(8,128)} %cot.1) | copy-start | bytes 3145732
  3.2 0.9 %copy-start.1 = (f32[1,8,4096]{2,1,0:T(8,128)S(1)}, f32[1,8,4096]{2,1,0:T(8,128)}, u32[]{:S(2)}) copy-start(f32[1,8,4096]{2,1,0:T(8,128)} %param.6) | copy-start | bytes 393220

commit v2 on v1

--- a/solution.py
+++ b/solution.py
@@ -114,7 +114,7 @@
 
 MESH = pl.DeviceIdType.MESH
 PAD = 128
-STRIP = 512
+STRIP = 4096
 
 
 def sincos(x):
@@ -188,7 +188,7 @@
 def fused(
     count, angles, order, slices, cot, out, grad,
     tmp, w2, w1, w0, field, full, sine, cosine, term, got, total, parts, rs, picks, gfull, pieces,
-    cot_send, cot_recv, cot_local, a2a_send, a2a_recv, ag_send, ag_recv, cx_send, cx_recv,
+    cot_send, cot_recv, cot_local, a2a_send, a2a_recv, a2a_local, ag_send, ag_recv, cx_send, cx_recv,
     tx_send, tx_recv, rs_send, rs_recv, fin_send, fin_recv, ex_send, ex_recv, ex_local,
 ):
     n = count
@@ -246,6 +246,9 @@
             (peer(k), core),
         )
 
+    def a2a_own():
+        return pltpu.make_async_copy(slices.at[:, my_cols], parts.at[me], a2a_local)
+
     def gather(layer, k):
         return remote(
             pieces.at[layer], full.at[layer, mine_rows, my_cols],
@@ -292,7 +295,7 @@
         cot_copy(g).start()
         cot_own(g).start()
     loop(lambda k: a2a(k).start())
-    parts[me] = slices[:, my_cols]
+    a2a_own().start()
     for g in range(held):
         for part in range(2):
             tmp[g, part, :, 0:PAD] = jnp.zeros((16, PAD), jnp.float32)
@@ -305,6 +308,7 @@
 
     back_first(0)
     loop(lambda k: a2a(k).wait_recv())
+    a2a_own().wait()
     for layer in range(layers - 1, -1, -1):
         value = parts[order[layer]]
         pieces[layer] = value
@@ -482,7 +486,7 @@
             jax.ShapeDtypeStruct(cotangent.shape, f32),
             jax.ShapeDtypeStruct((rows, cols), f32),
         ),
-        in_specs=[smem, smem, vmem, vmem],
+        in_specs=[smem, smem, pl.BlockSpec(memory_space=pl.ANY), pl.BlockSpec(memory_space=pl.ANY)],
         out_specs=(pl.BlockSpec(memory_space=pl.ANY), vmem),
         scratch_shapes=[
             pltpu.VMEM((held, 2, 2 * rows, cols + 2 * PAD), f32),
@@ -494,7 +498,7 @@
             pltpu.VMEM((rows, cols), f32),
             pltpu.VMEM((layers, rows, width), f32),
             dma((held,)), dma((held,)), dma((held,)),
-            dma((count,)), dma((count,)),
+            dma((count,)), dma((count,)), dma(()),
             dma((layers, count)), dma((layers, count)),
             dma((layers,)), dma((layers,)),
             dma((layers,)), dma((layers,)),
@@ -503,7 +507,7 @@
             dma((held,)), dma((held,)), dma((held,)),
         ],
         compiler_params=pltpu.CompilerParams(
-            collective_id=0, has_side_effects=True, vmem_limit_bytes=40 * 1024 * 1024
+            collective_id=0, has_side_effects=True, vmem_limit_bytes=56 * 1024 * 1024
         ),
     )(angles, depth_order, slices[0], cotangent)
     return out, grad[None]
@@ -521,7 +525,7 @@
         and depth_order.shape[0] == 3
         and cols & (cols - 1) == 0
         and cols % (128 * count) == 0
-        and cols % 512 == 0
+        and cols % STRIP == 0
     )
     run = fast_body if fits else body
     return run(angles, depth_order, slices, cotangent)

time: 69.1 us -> 56.3 us (0.81)
  Pallas kernels: 63.2 us -> 51.1 us
  local copies, waits for them, and re-layouts: 5.08 us -> 4.3 us
    pallas_call x1, Pallas kernels: 63.2 us -> 51.1 us  [fast_body(): pl.pallas_call(functools.partial(fused, count), out_shape=(jax.ShapeDtype...]
    unnamed x11 -> x7, local copies, waits for them, and re-layouts: 5.08 us -> 4.3 us
where the time goes in v2:
time: 56.3 us; the launch traced here: 56.1 us
  Pallas kernels  51.1 us (91%)
  local copies, waits for them, and re-layouts  4.3 us (8%)
  between operations  0.66 us (1%)
    pallas_call x1, Pallas kernels, fast_body(): pl.pallas_call(functools.partial(fused, count), out_shape=(jax.ShapeDtype...  51.1 us
    unnamed x7, local copies, waits for them, and re-layouts  4.3 us

profile of v2, /device:TPU:0, one launch (start us, length us, event | category | flops | bytes accessed | tf_op | source)
XLA Modules:
  0.0 56.1 jit_solution(14764904476766940802)
XLA Ops:
  0.6 0.0 copy-start.1
  0.6 0.7 %copy-done.1 = s32[4,2]{0,1:T(2,128)S(1)} copy-done((s32[4,2]{0,1:T(2,128)S(1)}, s32[4,2]{0,1:T(2,128)}, u32[]{:S(2)}) %copy-start.1) | copy-done | bytes 56
  1.3 0.7 %copy.6.angles = s32[4,2]{1,0:T(4,128)} copy(s32[4,2]{0,1:T(2,128)S(1)} %copy-done.1) | data formatting | bytes 64 | tf_op args[0]
  2.0 51.1 %shard_map.59 = (f32[4,2,8,4096]{3,2,1,0:T(8,128)}, f32[8,4096]{1,0:T(8,128)}) custom-call(s32[4,2]{1,0:T(4,128)} %copy.6.angles, s32[3]{0:T(128)} %order.1, f32[8,4096]{1,0:T(8,128)} %bitcast.2, f32[4,2,8,4096]{3,2,1,0:T(8,128)} %cot.1), custom_call_target="tpu_custom_call" | custom-call | tf_op jit(solution)/shard_map/pallas_call | solution.py:483
  53.1 0.0 copy-start
  53.1 2.3 %copy.9 = f32[4,2,8,4096]{3,2,1,0:T(8,128)} copy(f32[4,2,8,4096]{3,2,1,0:T(8,128)} %get-tuple-element.8) | data formatting | bytes 2097152
  55.4 0.0 copy-done
  55.4 0.7 %copy.10 = f32[1,8,4096]{2,1,0:T(8,128)} copy(f32[1,8,4096]{2,1,0:T(8,128)S(1)} %bitcast.3) | data formatting | bytes 262144
Async XLA Ops:
  0.6 0.7 %copy-start.1 = (s32[4,2]{0,1:T(2,128)S(1)}, s32[4,2]{0,1:T(2,128)}, u32[]{:S(2)}) copy-start(s32[4,2]{0,1:T(2,128)} %param.4) | copy-start | bytes 100
  53.1 2.3 %copy-start = (f32[8,4096]{1,0:T(8,128)S(1)}, f32[8,4096]{1,0:T(8,128)}, u32[]{:S(2)}) copy-start(f32[8,4096]{1,0:T(8,128)} %get-tuple-element.5) | copy-start | bytes 393220
